TPU v7x, 32 devices: a whole 2x2x4 slice. The times are simulated.
32 devices in a mesh: group: 2 (over x), atom: 4 (over y, core), layer: 4 (over z).
Axes of the slice: x: 2, y: 2, z: 4, core: 2. Of those that a mesh axis runs over, the one named last changes fastest.
Arguments:
- activations: bfloat16 [256, 4, 2304], P('group', 'layer'), parts along dimension 0, may hold values from -6 to 6
- encoder: bfloat16 [8, 2304, 16384], P(('group', 'layer'), None, 'atom'), parts along dimension 0, may hold values from -0.0625 to 0.0625
- decoder: bfloat16 [32768, 4, 2304], P(('group', 'atom'), 'layer'), parts along dimension 0, may hold values from -1 to 1
- thresholds: float32 [32768], P(('group', 'atom')), parts along dimension 0, may hold values from 0.05 to 0.8
Outputs:
- codes: bfloat16 [256, 16384], P('group', 'atom'), parts along dimension 0
- reconstruction: bfloat16 [256, 4, 2304], P(('group', 'atom'), 'layer'), parts along dimension 0
There are 2 independent parts, one for each index of `group`. A program takes and returns all parts, laid end to end along the dimension named above; each array names one. Nothing has to cross between parts.
All inputs are finite; a program needn't handle non-finite values.
Results may differ from a plain program's by a relative error of at most 0.02.
The roundings to bfloat16 on the way count: a program that leaves them out, or rounds other values in their place, can miss the bound.
Values may be sent and summed in bfloat16 or wider, within the bound.
A program may use at most 128 MiB of HBM per device.

v0:
```python
import jax
import jax.numpy as jnp
from jax import lax
from jax.sharding import PartitionSpec as P

REFINES = 2
step_rate = 0.15
learn_rate = 0.001


def shards(activations, encoder, decoder, thresholds):
    rows_in = activations[:, 0, :]
    enc_local = encoder[0]
    dec_local = decoder[:, 0, :]
    tokens = rows_in.shape[0]
    atom_devices = lax.axis_size("atom")

    def spread(code_state):
        return code_state.astype(jnp.bfloat16)

    def residual_of(coded_now, weights):
        row_count = tokens // atom_devices
        partial_value = lax.psum_scatter(
            jnp.dot(coded_now, weights, preferred_element_type=jnp.float32).astype(jnp.bfloat16),
            "atom",
            scatter_dimension=0,
            tiled=True,
        ).astype(jnp.float32)
        own_rows = lax.dynamic_slice_in_dim(
            rows_in, lax.axis_index("atom") * row_count, row_count, 0
        ).astype(jnp.float32)
        residual = lax.all_gather(
            (own_rows - partial_value).astype(jnp.bfloat16), "atom", axis=0, tiled=True
        )
        return (residual, False)

    def refine(code_state, coded_now, weights):
        residual, transposed = residual_of(coded_now, weights)
        gradient = lax.psum(
            lax.dot_general(
                residual, weights, (((1,), (1,)), ((), ())), preferred_element_type=jnp.float32
            ).astype(jnp.bfloat16),
            "layer",
        ).astype(jnp.float32)
        code_state = jax.nn.relu(code_state + step_rate * gradient - step_rate * thresholds)
        return (code_state, spread(code_state))

    preact = lax.psum(
        jnp.dot(rows_in, enc_local, preferred_element_type=jnp.float32).astype(jnp.bfloat16),
        "layer",
    ).astype(jnp.float32)
    code_state = jax.nn.relu(preact - thresholds)
    coded_now = spread(code_state)
    for sweep in range(REFINES):
        code_state, coded_now = refine(code_state, coded_now, dec_local)
    residual, transposed = residual_of(coded_now, dec_local)
    update = lax.dot_general(
        coded_now, residual, (((0,), (0,)), ((), ())), preferred_element_type=jnp.float32
    )
    renewed = (dec_local.astype(jnp.float32) + learn_rate * (update / tokens)).astype(jnp.bfloat16)
    code_state, coded_now = refine(code_state, coded_now, renewed)
    rebuilt = lax.psum_scatter(
        jnp.dot(coded_now, renewed, preferred_element_type=jnp.float32).astype(jnp.bfloat16),
        "atom",
        scatter_dimension=0,
        tiled=True,
    )
    reconstruction = rebuilt[:, None, :]
    return (coded_now, reconstruction)


def solution(mesh):
    return jax.shard_map(
        shards,
        mesh=mesh,
        in_specs=(
            P("group", "layer", None),
            P(("group", "layer"), None, "atom"),
            P(("group", "atom"), "layer", None),
            P(("group", "atom")),
        ),
        out_specs=(P("group", "atom"), P(("group", "atom"), "layer", None)),
        check_vma=False,
    )
```

profile of v0, /device:TPU:0, one launch (start us, length us, event | category | flops | bytes accessed | tf_op | source)
XLA Modules:
  0.0 487.0 jit_solution(16662554394716441295)
XLA Ops:
  7.2 0.0 all-reduce.5.cloned.1.call-start
  7.2 10.2 %fusion.12 = bf16[128,4096]{1,0:T(8,128)(2,1)} fusion(bf16[1,2304,4096]{2,1,0:T(8,128)(2,1)} %param.5, bf16[128,1,2304]{2,0,1:T(8,128)(2,1)} %param.4), kind=kOutput, calls=%fused_computation.13 | convolution fusion | flops 2416443392 | bytes 20512768 | tf_op jit(solution)/shard_map/dot_general | solution.py:49
  17.4 0.0 all-reduce.5.cloned.1.call-update
  17.4 0.0 reduce-scatter.6.cloned.1.call-start
  17.5 54.6 %all-reduce.5.cloned.1.call-done = bf16[128,4096]{1,0:T(8,128)(2,1)} async-done(((bf16[128,4096]{1,0:T(8,128)(2,1)}), bf16[128,4096]{1,0:T(8,128)(2,1)}) %all-reduce.5.cloned.1.call-update) | async-done | bytes 1048592 | tf_op jit(solution)/shard_map/psum | solution.py:48
  72.1 10.1 %fusion.21 = bf16[128,2304]{1,0:T(8,128)(2,1)} fusion(bf16[4096,1,2304]{2,0,1:T(8,128)(2,1)} %param.6, bf16[128,4096]{1,0:T(8,128)(2,1)} %all-reduce.5.cloned.1.call-done, f32[4096]{0:T(1024)S(1)} %copy-done.4), kind=kOutput, calls=%fused_computation.17 | convolution fusion | flops 2418311168 | bytes 20529152 | tf_op jit(solution)/shard_map/dot_general | solution.py:24
  82.2 0.0 reduce-scatter.6.cloned.1.call-update
  82.3 0.0 all-reduce.7.cloned.1.call-start
  82.3 21.6 %reduce-scatter.6.cloned.1.call-done = bf16[32,2304]{1,0:T(8,128)(2,1)} async-done(((bf16[128,2304]{1,0:T(8,128)(2,1)}), bf16[32,2304]{1,0:T(8,128)(2,1)}) %reduce-scatter.6.cloned.1.call-update) | async-done | bytes 147472 | tf_op jit(solution)/shard_map/reduce_scatter | solution.py:23
  103.9 0.9 fusion.42
  104.8 7.1 %all_gather.12 = bf16[128,2304]{1,0:T(8,128)(2,1)S(1)} all-gather(bf16[32,2304]{1,0:T(8,128)(2,1)S(1)} %fusion.42), channel_id=1, replica_groups=mesh['group'=2,'atom'=4,'layer'=4] {'atom'}, dimensions={0}, use_global_device_ids=true | all-gather | bytes 737280 | tf_op jit(solution)/shard_map/all_gather | solution.py:32
  112.0 13.6 %fusion.15 = bf16[128,4096]{1,0:T(8,128)(2,1)} fusion(bf16[128,2304]{1,0:T(8,128)(2,1)S(1)} %all_gather.12, bf16[4096,1,2304]{2,0,1:T(8,128)(2,1)} %param.6), kind=kOutput, calls=%fused_computation.14 | convolution fusion | flops 2416443392 | bytes 20512768 | tf_op jit(solution)/shard_map/dot_general | solution.py:40
  125.5 0.0 all-reduce.7.cloned.1.call-update
  125.5 0.0 reduce-scatter.8.cloned.1.call-start
  125.6 52.3 %all-reduce.7.cloned.1.call-done = bf16[128,4096]{1,0:T(8,128)(2,1)} async-done(((bf16[128,4096]{1,0:T(8,128)(2,1)}), bf16[128,4096]{1,0:T(8,128)(2,1)}) %all-reduce.7.cloned.1.call-update) | async-done | bytes 1048592 | tf_op jit(solution)/shard_map/psum | solution.py:39
  177.9 10.4 %fusion.24 = bf16[128,2304]{1,0:T(8,128)(2,1)} fusion(bf16[4096,1,2304]{2,0,1:T(8,128)(2,1)} %param.6, bf16[128,4096]{1,0:T(8,128)(2,1)} %all-reduce.7.cloned.1.call-done, bf16[128,4096]{1,0:T(8,128)(2,1)S(1)} %copy-done, f32[4096]{0:T(1024)S(1)} %broadcast_multiply_fusion, f32[4096]{0:T(1024)S(1)} %copy-done.4), kind=kOutput, calls=%fused_computation.18 | convolution fusion | flops 2420932608 | bytes 21594112 | tf_op jit(solution)/shard_map/dot_general | solution.py:24
  188.3 0.0 reduce-scatter.8.cloned.1.call-update
  188.3 0.0 all-reduce.9.cloned.1.call-start
  188.4 21.5 %reduce-scatter.8.cloned.1.call-done = bf16[32,2304]{1,0:T(8,128)(2,1)} async-done(((bf16[128,2304]{1,0:T(8,128)(2,1)}), bf16[32,2304]{1,0:T(8,128)(2,1)}) %reduce-scatter.8.cloned.1.call-update) | async-done | bytes 147472 | tf_op jit(solution)/shard_map/reduce_scatter | solution.py:23
  209.9 0.9 fusion.43
  210.9 7.3 %all_gather.13 = bf16[128,2304]{1,0:T(8,128)(2,1)S(1)} all-gather(bf16[32,2304]{1,0:T(8,128)(2,1)S(1)} %fusion.43), channel_id=1, replica_groups=mesh['group'=2,'atom'=4,'layer'=4] {'atom'}, dimensions={0}, use_global_device_ids=true | all-gather | bytes 737280 | tf_op jit(solution)/shard_map/all_gather | solution.py:32
  218.2 13.6 %fusion.18 = bf16[128,4096]{1,0:T(8,128)(2,1)} fusion(bf16[128,2304]{1,0:T(8,128)(2,1)S(1)} %all_gather.13, bf16[4096,1,2304]{2,0,1:T(8,128)(2,1)} %param.6), kind=kOutput, calls=%fused_computation.15 | convolution fusion | flops 2416443392 | bytes 20512768 | tf_op jit(solution)/shard_map/dot_general | solution.py:40
  231.8 0.0 all-reduce.9.cloned.1.call-update
  231.8 0.0 reduce-scatter.10.cloned.1.call-start
  231.8 52.3 %all-reduce.9.cloned.1.call-done = bf16[128,4096]{1,0:T(8,128)(2,1)} async-done(((bf16[128,4096]{1,0:T(8,128)(2,1)}), bf16[128,4096]{1,0:T(8,128)(2,1)}) %all-reduce.9.cloned.1.call-update) | async-done | bytes 1048592 | tf_op jit(solution)/shard_map/psum | solution.py:39
  284.2 2.1 fusion.41
  286.3 9.8 %fusion.27 = bf16[128,2304]{1,0:T(8,128)(2,1)} fusion(bf16[128,4096]{1,0:T(8,128)(2,1)S(1)} %fusion.41, bf16[4096,1,2304]{2,0,1:T(8,128)(2,1)} %param.6), kind=kOutput, calls=%fused_computation.19 | convolution fusion | flops 2416214016 | bytes 20512768 | tf_op jit(solution)/shard_map/dot_general | solution.py:24
  296.1 0.0 reduce-scatter.10.cloned.1.call-update
  296.1 0.0 reduce-scatter.12.cloned.1.call-start
  296.2 21.6 %reduce-scatter.10.cloned.1.call-done = bf16[32,2304]{1,0:T(8,128)(2,1)} async-done(((bf16[128,2304]{1,0:T(8,128)(2,1)}), bf16[32,2304]{1,0:T(8,128)(2,1)}) %reduce-scatter.10.cloned.1.call-update) | async-done | bytes 147472 | tf_op jit(solution)/shard_map/reduce_scatter | solution.py:23
  317.8 1.0 fusion.44
  318.8 7.8 %all_gather.14 = bf16[128,2304]{1,0:T(8,128)(2,1)} all-gather(bf16[32,2304]{1,0:T(8,128)(2,1)S(1)} %fusion.44), channel_id=1, replica_groups=mesh['group'=2,'atom'=4,'layer'=4] {'atom'}, dimensions={0}, use_global_device_ids=true | all-gather | bytes 737280 | tf_op jit(solution)/shard_map/all_gather | solution.py:32
  326.6 12.9 %add_convert_fusion = bf16[4096,2304]{1,0:T(8,128)(2,1)} fusion(bf16[128,4096]{1,0:T(8,128)(2,1)S(1)} %fusion.41, bf16[128,2304]{1,0:T(8,128)(2,1)} %all_gather.14, bf16[4096,1,2304]{2,0,1:T(8,128)(2,1)} %param.6), kind=kOutput, calls=%fused_computation | convolution fusion | flops 2453667840 | bytes 39387136 | tf_op jit(solution)/shard_map/dot_general | solution.py:57
  339.4 9.8 %convolution_convert_fusion.2 = bf16[128,2304]{1,0:T(8,128)(2,1)} fusion(bf16[128,4096]{1,0:T(8,128)(2,1)S(1)} %fusion.41, bf16[4096,2304]{1,0:T(8,128)(2,1)} %add_convert_fusion), kind=kOutput, calls=%fused_computation.21 | convolution fusion | flops 2416214016 | bytes 20512768 | tf_op jit(solution)/shard_map/dot_general | solution.py:24
  349.2 0.0 reduce-scatter.12.cloned.1.call-update
  349.3 0.0 all-reduce.11.cloned.1.call-start
  349.3 22.6 %reduce-scatter.12.cloned.1.call-done = bf16[32,2304]{1,0:T(8,128)(2,1)} async-done(((bf16[128,2304]{1,0:T(8,128)(2,1)}), bf16[32,2304]{1,0:T(8,128)(2,1)}) %reduce-scatter.12.cloned.1.call-update) | async-done | bytes 147472 | tf_op jit(solution)/shard_map/reduce_scatter | solution.py:23
  371.9 1.0 fusion.45
  372.9 7.1 %all_gather.15 = bf16[128,2304]{1,0:T(8,128)(2,1)S(1)} all-gather(bf16[32,2304]{1,0:T(8,128)(2,1)S(1)} %fusion.45), channel_id=1, replica_groups=mesh['group'=2,'atom'=4,'layer'=4] {'atom'}, dimensions={0}, use_global_device_ids=true | all-gather | bytes 737280 | tf_op jit(solution)/shard_map/all_gather | solution.py:32
  380.0 13.5 %convolution_convert_fusion = bf16[128,4096]{1,0:T(8,128)(2,1)} fusion(bf16[128,2304]{1,0:T(8,128)(2,1)S(1)} %all_gather.15, bf16[4096,2304]{1,0:T(8,128)(2,1)} %add_convert_fusion), kind=kOutput, calls=%fused_computation.16 | convolution fusion | flops 2416443392 | bytes 20512768 | tf_op jit(solution)/shard_map/dot_general | solution.py:40
  393.5 0.0 all-reduce.11.cloned.1.call-update
  393.5 0.3 reduce-scatter.14.cloned.1.call-start
  393.8 52.0 %all-reduce.11.cloned.1.call-done = bf16[128,4096]{1,0:T(8,128)(2,1)} async-done(((bf16[128,4096]{1,0:T(8,128)(2,1)}), bf16[128,4096]{1,0:T(8,128)(2,1)}) %all-reduce.11.cloned.1.call-update) | async-done | bytes 1048592 | tf_op jit(solution)/shard_map/psum | solution.py:39
  445.9 2.8 maximum_convert_fusion
  448.7 0.0 copy-start.1
  448.7 10.2 %convolution_convert_fusion.1 = bf16[128,2304]{1,0:T(8,128)(2,1)} fusion(bf16[128,4096]{1,0:T(8,128)(2,1)S(1)} %maximum_convert_fusion, bf16[4096,2304]{1,0:T(8,128)(2,1)} %add_convert_fusion), kind=kOutput, calls=%fused_computation.20 | convolution fusion | flops 2416214016 | bytes 20512768 | tf_op jit(solution)/shard_map/dot_general | solution.py:63
  458.9 0.0 reduce-scatter.14.cloned.1.call-update
  458.9 21.6 %reduce-scatter.14.cloned.1.call-done = bf16[32,2304]{1,0:T(8,128)(2,1)} async-done(((bf16[128,2304]{1,0:T(8,128)(2,1)}), bf16[32,2304]{1,0:T(8,128)(2,1)}) %reduce-scatter.14.cloned.1.call-update) | async-done | bytes 147472 | tf_op jit(solution)/shard_map/reduce_scatter | solution.py:62
  (10 shorter events, 0.0 us)
Async XLA Ops:
  7.2 64.9 %copy-start.4 = (f32[4096]{0:T(1024)S(1)}, f32[4096]{0:T(1024)}, u32[]{:S(2)}) copy-start(f32[4096]{0:T(1024)} %param.7) | copy-start | bytes 49156
  7.2 64.9 %all-reduce.5.cloned.1.call-start = ((), (), s32[]{:S(2)}) async-start(), calls=%async_computation.5 | async-start | bytes 2097152 | tf_op jit(solution)/shard_map/psum | solution.py:48
  17.4 86.5 %copy-start.3 = (bf16[128,1,2304]{2,0,1:T(8,128)(2,1)S(1)}, bf16[128,1,2304]{2,0,1:T(8,128)(2,1)}, u32[]{:S(2)}) copy-start(bf16[128,1,2304]{2,0,1:T(8,128)(2,1)} %param.4) | copy-start | bytes 1769476
  17.4 86.5 %reduce-scatter.6.cloned.1.call-start = ((), (), s32[]{:S(2)}) async-start(), calls=%async_computation.6 | async-start | bytes 737280 | tf_op jit(solution)/shard_map/reduce_scatter | solution.py:23
  82.3 95.6 %all-reduce.7.cloned.1.call-start = ((), (), s32[]{:S(2)}) async-start(), calls=%async_computation.7 | async-start | bytes 2097152 | tf_op jit(solution)/shard_map/psum | solution.py:39
  112.0 65.9 %copy-start = (bf16[128,4096]{1,0:T(8,128)(2,1)S(1)}, bf16[128,4096]{1,0:T(8,128)(2,1)}, u32[]{:S(2)}) copy-start(bf16[128,4096]{1,0:T(8,128)(2,1)} %all-reduce.5.cloned.1.call-done) | copy-start | bytes 3145732
  125.5 84.4 %reduce-scatter.8.cloned.1.call-start = ((), (), s32[]{:S(2)}) async-start(), calls=%async_computation.8 | async-start | bytes 737280 | tf_op jit(solution)/shard_map/reduce_scatter | solution.py:23
  188.3 95.8 %all-reduce.9.cloned.1.call-start = ((), (), s32[]{:S(2)}) async-start(), calls=%async_computation.9 | async-start | bytes 2097152 | tf_op jit(solution)/shard_map/psum | solution.py:39
  218.2 65.9 %copy-start.2 = (bf16[128,4096]{1,0:T(8,128)(2,1)S(1)}, bf16[128,4096]{1,0:T(8,128)(2,1)}, u32[]{:S(2)}) copy-start(bf16[128,4096]{1,0:T(8,128)(2,1)} %all-reduce.7.cloned.1.call-done) | copy-start | bytes 3145732
  231.8 86.0 %reduce-scatter.10.cloned.1.call-start = ((), (), s32[]{:S(2)}) async-start(), calls=%async_computation.10 | async-start | bytes 737280 | tf_op jit(solution)/shard_map/reduce_scatter | solution.py:23
  296.1 75.8 %reduce-scatter.12.cloned.1.call-start = ((), (), s32[]{:S(2)}) async-start(), calls=%async_computation.11 | async-start | bytes 737280 | tf_op jit(solution)/shard_map/reduce_scatter | solution.py:23
  349.3 96.6 %all-reduce.11.cloned.1.call-start = ((), (), s32[]{:S(2)}) async-start(), calls=%async_computation.12 | async-start | bytes 2097152 | tf_op jit(solution)/shard_map/psum | solution.py:39
  393.5 87.0 %reduce-scatter.14.cloned.1.call-start = ((), (), s32[]{:S(2)}) async-start(), calls=%async_computation.13 | async-start | bytes 737280 | tf_op jit(solution)/shard_map/reduce_scatter | solution.py:62
  448.7 10.2 %copy-start.1 = (bf16[128,4096]{1,0:T(8,128)(2,1)}, bf16[128,4096]{1,0:T(8,128)(2,1)S(1)}, u32[]{:S(2)}) copy-start(bf16[128,4096]{1,0:T(8,128)(2,1)S(1)} %maximum_convert_fusion) | copy-start | bytes 3145732
Sparse Core Ops, SparseCore 0:
  17.5 54.5 all-reduce.4
  82.4 21.4 reduce-scatter.5
  125.7 52.1 all-reduce.6
  188.5 21.4 reduce-scatter.7
  231.9 52.1 all-reduce.8
  296.2 21.4 reduce-scatter.9
  349.4 22.4 reduce-scatter.11
  393.6 52.1 all-reduce.10
  459.0 21.4 reduce-scatter.13
where the time goes:
time: 488 us; the launch traced here: 487 us
  waiting for transfers between devices  320 us (66%)
  matrix products  114 us (23%)
  blocking collectives  29.4 us (6%)
  between operations  13.9 us (3%)
  other arithmetic  8.87 us (2%)
    psum x3, waiting for transfers between devices, refine(): lax.psum(lax.dot_general(residual, weights, (((1,), (1,)), ((), ())), pre...  157 us
    reduce_scatter x4, waiting for transfers between devices, residual_of(): lax.psum_scatter(jnp.dot(coded_now, weights, preferred_element_type=jnp.f...  87.3 us
    psum x1, waiting for transfers between devices, shards(): lax.psum(jnp.dot(rows_in, enc_local, preferred_element_type=jnp.float32)....  54.6 us
    dot_general x3, matrix products, refine(): lax.dot_general(residual, weights, (((1,), (1,)), ((), ())), preferred_el...  40.6 us
    dot_general x4, matrix products, residual_of(): jnp.dot(coded_now, weights, preferred_element_type=jnp.float32)  40.2 us
    all_gather x4, blocking collectives, residual_of(): lax.all_gather((own_rows - partial_value).astype(jnp.bfloat16), 'atom', a...  29.4 us
    reduce_scatter x1, waiting for transfers between devices, shards(): lax.psum_scatter(jnp.dot(coded_now, renewed, preferred_element_type=jnp.f...  21.6 us
    dot_general x1, matrix products, shards(): lax.dot_general(coded_now, residual, (((0,), (0,)), ((), ())), preferred_...  12.9 us
  transfers between devices with their start and end apart: 9, of which 9 were waited for; matrix products, arithmetic and copies ran while one was open for 0% of the time, Pallas kernels for 0%

commit v1 on v0

--- a/solution.py
+++ b/solution.py
@@ -45,9 +45,12 @@
         code_state = jax.nn.relu(code_state + step_rate * gradient - step_rate * thresholds)
         return (code_state, spread(code_state))
 
-    preact = lax.psum(
-        jnp.dot(rows_in, enc_local, preferred_element_type=jnp.float32).astype(jnp.bfloat16),
-        "layer",
+    preact = jnp.sum(
+        lax.all_gather(
+            jnp.dot(rows_in, enc_local, preferred_element_type=jnp.float32).astype(jnp.bfloat16),
+            "layer",
+        ),
+        axis=0,
     ).astype(jnp.float32)
     code_state = jax.nn.relu(preact - thresholds)
     coded_now = spread(code_state)

time: 488 us -> 518 us (1.061)
  waiting for transfers between devices: 320 us -> 348 us
    all_gather x0 -> x1, waiting for transfers between devices: none -> 83.6 us  [shards(): lax.all_gather(jnp.dot(rows_in, enc_local, preferred_element_type=jnp.flo...]
    psum x1 -> x0, waiting for transfers between devices: 54.6 us -> none  [shards(): lax.psum(jnp.dot(rows_in, enc_local, preferred_element_type=jnp.float32)....]
where the time goes in v1:
time: 518 us
  waiting for transfers between devices  348 us (67%)
  matrix products  114 us (22%)
  blocking collectives  29.2 us (6%)
  between operations  13.9 us (3%)
  other arithmetic  11.9 us (2%)
    psum x3, waiting for transfers between devices, refine(): lax.psum(lax.dot_general(residual, weights, (((1,), (1,)), ((), ())), pre...  156 us
    reduce_scatter x4, waiting for transfers between devices, residual_of(): lax.psum_scatter(jnp.dot(coded_now, weights, preferred_element_type=jnp.f...  86.3 us
    all_gather x1, waiting for transfers between devices, shards(): lax.all_gather(jnp.dot(rows_in, enc_local, preferred_element_type=jnp.flo...  83.6 us
    dot_general x3, matrix products, refine(): lax.dot_general(residual, weights, (((1,), (1,)), ((), ())), preferred_el...  40.5 us
    dot_general x4, matrix products, residual_of(): jnp.dot(coded_now, weights, preferred_element_type=jnp.float32)  39.9 us
    all_gather x4, blocking collectives, residual_of(): lax.all_gather((own_rows - partial_value).astype(jnp.bfloat16), 'atom', a...  29.2 us
    reduce_scatter x1, waiting for transfers between devices, shards(): lax.psum_scatter(jnp.dot(coded_now, renewed, preferred_element_type=jnp.f...  21.6 us
    dot_general x1, matrix products, shards(): lax.dot_general(coded_now, residual, (((0,), (0,)), ((), ())), preferred_...  12.9 us
  transfers between devices with their start and end apart: 9, of which 9 were waited for; matrix products, arithmetic and copies ran while one was open for 0% of the time, Pallas kernels for 0%

profile of v1, /device:TPU:0, one launch (start us, length us, event | category | flops | bytes accessed | tf_op | source)
XLA Modules:
  0.0 517.7 jit_solution(11319858499886546206)
XLA Ops:
  7.2 0.0 all-gather.3.cloned.1.call-start
  7.2 10.2 %fusion.12 = bf16[128,4096]{1,0:T(8,128)(2,1)} fusion(bf16[1,2304,4096]{2,1,0:T(8,128)(2,1)} %param.5, bf16[128,1,2304]{2,0,1:T(8,128)(2,1)} %param.4), kind=kOutput, calls=%fused_computation.13 | convolution fusion | flops 2416443392 | bytes 20512768 | tf_op jit(solution)/shard_map/dot_general | solution.py:50
  17.4 0.0 all-gather.3.cloned.1.call-update
  17.4 0.0 reduce-scatter.6.cloned.1.call-start
  17.4 83.6 %all-gather.3.cloned.1.call-done = bf16[512,4096]{1,0:T(8,128)(2,1)} async-done(((bf16[128,4096]{1,0:T(8,128)(2,1)}), bf16[512,4096]{1,0:T(8,128)(2,1)}) %all-gather.3.cloned.1.call-update) | async-done | bytes 4194320 | tf_op jit(solution)/shard_map/all_gather | solution.py:49
  101.0 3.1 reduce_sum.12
  104.1 9.9 %fusion.21 = bf16[128,2304]{1,0:T(8,128)(2,1)} fusion(bf16[4096,1,2304]{2,0,1:T(8,128)(2,1)} %param.6, bf16[128,4096]{1,0:T(8,128)(2,1)S(1)} %reduce_sum.12, f32[4096]{0:T(1024)S(1)} %copy-done.3), kind=kOutput, calls=%fused_computation.17 | convolution fusion | flops 2418311168 | bytes 20529152 | tf_op jit(solution)/shard_map/dot_general | solution.py:24
  114.0 0.0 reduce-scatter.6.cloned.1.call-update
  114.0 0.0 all-reduce.4.cloned.1.call-start
  114.1 20.7 %reduce-scatter.6.cloned.1.call-done = bf16[32,2304]{1,0:T(8,128)(2,1)} async-done(((bf16[128,2304]{1,0:T(8,128)(2,1)}), bf16[32,2304]{1,0:T(8,128)(2,1)}) %reduce-scatter.6.cloned.1.call-update) | async-done | bytes 147472 | tf_op jit(solution)/shard_map/reduce_scatter | solution.py:23
  134.8 0.9 fusion.42
  135.7 7.1 %all_gather.20 = bf16[128,2304]{1,0:T(8,128)(2,1)S(1)} all-gather(bf16[32,2304]{1,0:T(8,128)(2,1)S(1)} %fusion.42), channel_id=1, replica_groups=mesh['group'=2,'atom'=4,'layer'=4] {'atom'}, dimensions={0}, use_global_device_ids=true | all-gather | bytes 737280 | tf_op jit(solution)/shard_map/all_gather | solution.py:32
  142.9 13.4 %fusion.15 = bf16[128,4096]{1,0:T(8,128)(2,1)} fusion(bf16[128,2304]{1,0:T(8,128)(2,1)S(1)} %all_gather.20, bf16[4096,1,2304]{2,0,1:T(8,128)(2,1)} %param.6), kind=kOutput, calls=%fused_computation.14 | convolution fusion | flops 2416443392 | bytes 20512768 | tf_op jit(solution)/shard_map/dot_general | solution.py:40
  156.3 0.0 all-reduce.4.cloned.1.call-update
  156.3 0.2 reduce-scatter.8.cloned.1.call-start
  156.6 52.1 %all-reduce.4.cloned.1.call-done = bf16[128,4096]{1,0:T(8,128)(2,1)} async-done(((bf16[128,4096]{1,0:T(8,128)(2,1)}), bf16[128,4096]{1,0:T(8,128)(2,1)}) %all-reduce.4.cloned.1.call-update) | async-done | bytes 1048592 | tf_op jit(solution)/shard_map/psum | solution.py:39
  208.7 10.4 %fusion.24 = bf16[128,2304]{1,0:T(8,128)(2,1)} fusion(bf16[4096,1,2304]{2,0,1:T(8,128)(2,1)} %param.6, bf16[128,4096]{1,0:T(8,128)(2,1)} %all-reduce.4.cloned.1.call-done, bf16[128,4096]{1,0:T(8,128)(2,1)S(1)} %reduce_sum.12, f32[4096]{0:T(1024)S(1)} %broadcast_multiply_fusion, f32[4096]{0:T(1024)S(1)} %copy-done.3), kind=kOutput, calls=%fused_computation.18 | convolution fusion | flops 2420932608 | bytes 21594112 | tf_op jit(solution)/shard_map/dot_general | solution.py:24
  219.1 0.0 reduce-scatter.8.cloned.1.call-update
  219.2 0.0 all-reduce.6.cloned.1.call-start
  219.2 21.6 %reduce-scatter.8.cloned.1.call-done = bf16[32,2304]{1,0:T(8,128)(2,1)} async-done(((bf16[128,2304]{1,0:T(8,128)(2,1)}), bf16[32,2304]{1,0:T(8,128)(2,1)}) %reduce-scatter.8.cloned.1.call-update) | async-done | bytes 147472 | tf_op jit(solution)/shard_map/reduce_scatter | solution.py:23
  240.8 0.9 fusion.43
  241.7 7.1 %all_gather.21 = bf16[128,2304]{1,0:T(8,128)(2,1)S(1)} all-gather(bf16[32,2304]{1,0:T(8,128)(2,1)S(1)} %fusion.43), channel_id=1, replica_groups=mesh['group'=2,'atom'=4,'layer'=4] {'atom'}, dimensions={0}, use_global_device_ids=true | all-gather | bytes 737280 | tf_op jit(solution)/shard_map/all_gather | solution.py:32
  248.9 13.6 %fusion.18 = bf16[128,4096]{1,0:T(8,128)(2,1)} fusion(bf16[128,2304]{1,0:T(8,128)(2,1)S(1)} %all_gather.21, bf16[4096,1,2304]{2,0,1:T(8,128)(2,1)} %param.6), kind=kOutput, calls=%fused_computation.15 | convolution fusion | flops 2416443392 | bytes 20512768 | tf_op jit(solution)/shard_map/dot_general | solution.py:40
  262.4 0.0 all-reduce.6.cloned.1.call-update
  262.4 0.0 reduce-scatter.10.cloned.1.call-start
  262.5 52.3 %all-reduce.6.cloned.1.call-done = bf16[128,4096]{1,0:T(8,128)(2,1)} async-done(((bf16[128,4096]{1,0:T(8,128)(2,1)}), bf16[128,4096]{1,0:T(8,128)(2,1)}) %all-reduce.6.cloned.1.call-update) | async-done | bytes 1048592 | tf_op jit(solution)/shard_map/psum | solution.py:39
  314.8 2.1 fusion.41
  316.9 9.8 %fusion.27 = bf16[128,2304]{1,0:T(8,128)(2,1)} fusion(bf16[128,4096]{1,0:T(8,128)(2,1)S(1)} %fusion.41, bf16[4096,1,2304]{2,0,1:T(8,128)(2,1)} %param.6), kind=kOutput, calls=%fused_computation.19 | convolution fusion | flops 2416214016 | bytes 20512768 | tf_op jit(solution)/shard_map/dot_general | solution.py:24
  326.7 0.0 reduce-scatter.10.cloned.1.call-update
  326.8 0.0 reduce-scatter.12.cloned.1.call-start
  326.8 21.5 %reduce-scatter.10.cloned.1.call-done = bf16[32,2304]{1,0:T(8,128)(2,1)} async-done(((bf16[128,2304]{1,0:T(8,128)(2,1)}), bf16[32,2304]{1,0:T(8,128)(2,1)}) %reduce-scatter.10.cloned.1.call-update) | async-done | bytes 147472 | tf_op jit(solution)/shard_map/reduce_scatter | solution.py:23
  348.4 1.0 fusion.44
  349.4 7.8 %all_gather.22 = bf16[128,2304]{1,0:T(8,128)(2,1)} all-gather(bf16[32,2304]{1,0:T(8,128)(2,1)S(1)} %fusion.44), channel_id=1, replica_groups=mesh['group'=2,'atom'=4,'layer'=4] {'atom'}, dimensions={0}, use_global_device_ids=true | all-gather | bytes 737280 | tf_op jit(solution)/shard_map/all_gather | solution.py:32
  357.2 12.9 %add_convert_fusion = bf16[4096,2304]{1,0:T(8,128)(2,1)} fusion(bf16[128,4096]{1,0:T(8,128)(2,1)S(1)} %fusion.41, bf16[128,2304]{1,0:T(8,128)(2,1)} %all_gather.22, bf16[4096,1,2304]{2,0,1:T(8,128)(2,1)} %param.6), kind=kOutput, calls=%fused_computation | convolution fusion | flops 2453667840 | bytes 39387136 | tf_op jit(solution)/shard_map/dot_general | solution.py:60
  370.1 9.8 %convolution_convert_fusion.2 = bf16[128,2304]{1,0:T(8,128)(2,1)} fusion(bf16[128,4096]{1,0:T(8,128)(2,1)S(1)} %fusion.41, bf16[4096,2304]{1,0:T(8,128)(2,1)} %add_convert_fusion), kind=kOutput, calls=%fused_computation.21 | convolution fusion | flops 2416214016 | bytes 20512768 | tf_op jit(solution)/shard_map/dot_general | solution.py:24
  379.9 0.0 reduce-scatter.12.cloned.1.call-update
  379.9 0.0 all-reduce.8.cloned.1.call-start
  379.9 22.5 %reduce-scatter.12.cloned.1.call-done = bf16[32,2304]{1,0:T(8,128)(2,1)} async-done(((bf16[128,2304]{1,0:T(8,128)(2,1)}), bf16[32,2304]{1,0:T(8,128)(2,1)}) %reduce-scatter.12.cloned.1.call-update) | async-done | bytes 147472 | tf_op jit(solution)/shard_map/reduce_scatter | solution.py:23
  402.5 1.0 fusion.45
  403.5 7.1 %all_gather.23 = bf16[128,2304]{1,0:T(8,128)(2,1)S(1)} all-gather(bf16[32,2304]{1,0:T(8,128)(2,1)S(1)} %fusion.45), channel_id=1, replica_groups=mesh['group'=2,'atom'=4,'layer'=4] {'atom'}, dimensions={0}, use_global_device_ids=true | all-gather | bytes 737280 | tf_op jit(solution)/shard_map/all_gather | solution.py:32
  410.6 13.5 %convolution_convert_fusion = bf16[128,4096]{1,0:T(8,128)(2,1)} fusion(bf16[128,2304]{1,0:T(8,128)(2,1)S(1)} %all_gather.23, bf16[4096,2304]{1,0:T(8,128)(2,1)} %add_convert_fusion), kind=kOutput, calls=%fused_computation.16 | convolution fusion | flops 2416443392 | bytes 20512768 | tf_op jit(solution)/shard_map/dot_general | solution.py:40
  424.1 0.0 all-reduce.8.cloned.1.call-update
  424.1 0.3 reduce-scatter.14.cloned.1.call-start
  424.4 52.0 %all-reduce.8.cloned.1.call-done = bf16[128,4096]{1,0:T(8,128)(2,1)} async-done(((bf16[128,4096]{1,0:T(8,128)(2,1)}), bf16[128,4096]{1,0:T(8,128)(2,1)}) %all-reduce.8.cloned.1.call-update) | async-done | bytes 1048592 | tf_op jit(solution)/shard_map/psum | solution.py:39
  476.5 2.8 maximum_convert_fusion
  479.3 10.2 %convolution_convert_fusion.1 = bf16[128,2304]{1,0:T(8,128)(2,1)} fusion(bf16[128,4096]{1,0:T(8,128)(2,1)S(1)} %maximum_convert_fusion, bf16[4096,2304]{1,0:T(8,128)(2,1)} %add_convert_fusion), kind=kOutput, calls=%fused_computation.20 | convolution fusion | flops 2416214016 | bytes 20512768 | tf_op jit(solution)/shard_map/dot_general | solution.py:66
  489.5 0.0 reduce-scatter.14.cloned.1.call-update
  489.5 21.6 %reduce-scatter.14.cloned.1.call-done = bf16[32,2304]{1,0:T(8,128)(2,1)} async-done(((bf16[128,2304]{1,0:T(8,128)(2,1)}), bf16[32,2304]{1,0:T(8,128)(2,1)}) %reduce-scatter.14.cloned.1.call-update) | async-done | bytes 147472 | tf_op jit(solution)/shard_map/reduce_scatter | solution.py:65
  (9 shorter events, 0.0 us)
Async XLA Ops:
  7.2 93.8 %all-gather.3.cloned.1.call-start = ((), (), s32[]{:S(2)}) async-start(), calls=%async_computation.13 | async-start | bytes 5242880 | tf_op jit(solution)/shard_map/all_gather | solution.py:49
  17.4 117.4 %reduce-scatter.6.cloned.1.call-start = ((), (), s32[]{:S(2)}) async-start(), calls=%async_computation.5 | async-start | bytes 737280 | tf_op jit(solution)/shard_map/reduce_scatter | solution.py:23
  101.0 3.1 copy-start.3
  104.1 30.7 %copy-start.2 = (bf16[128,1,2304]{2,0,1:T(8,128)(2,1)S(1)}, bf16[128,1,2304]{2,0,1:T(8,128)(2,1)}, u32[]{:S(2)}) copy-start(bf16[128,1,2304]{2,0,1:T(8,128)(2,1)} %param.4) | copy-start | bytes 1769476
  114.0 94.7 %all-reduce.4.cloned.1.call-start = ((), (), s32[]{:S(2)}) async-start(), calls=%async_computation.6 | async-start | bytes 2097152 | tf_op jit(solution)/shard_map/psum | solution.py:39
  156.3 84.4 %reduce-scatter.8.cloned.1.call-start = ((), (), s32[]{:S(2)}) async-start(), calls=%async_computation.7 | async-start | bytes 737280 | tf_op jit(solution)/shard_map/reduce_scatter | solution.py:23
  219.2 95.6 %all-reduce.6.cloned.1.call-start = ((), (), s32[]{:S(2)}) async-start(), calls=%async_computation.8 | async-start | bytes 2097152 | tf_op jit(solution)/shard_map/psum | solution.py:39
  248.8 65.9 %copy-start.1 = (bf16[128,4096]{1,0:T(8,128)(2,1)S(1)}, bf16[128,4096]{1,0:T(8,128)(2,1)}, u32[]{:S(2)}) copy-start(bf16[128,4096]{1,0:T(8,128)(2,1)} %all-reduce.4.cloned.1.call-done) | copy-start | bytes 3145732
  262.4 85.9 %reduce-scatter.10.cloned.1.call-start = ((), (), s32[]{:S(2)}) async-start(), calls=%async_computation.9 | async-start | bytes 737280 | tf_op jit(solution)/shard_map/reduce_scatter | solution.py:23
  326.8 75.7 %reduce-scatter.12.cloned.1.call-start = ((), (), s32[]{:S(2)}) async-start(), calls=%async_computation.10 | async-start | bytes 737280 | tf_op jit(solution)/shard_map/reduce_scatter | solution.py:23
  379.9 96.6 %all-reduce.8.cloned.1.call-start = ((), (), s32[]{:S(2)}) async-start(), calls=%async_computation.11 | async-start | bytes 2097152 | tf_op jit(solution)/shard_map/psum | solution.py:39
  424.1 87.0 %reduce-scatter.14.cloned.1.call-start = ((), (), s32[]{:S(2)}) async-start(), calls=%async_computation.12 | async-start | bytes 737280 | tf_op jit(solution)/shard_map/reduce_scatter | solution.py:65
  479.3 10.2 %copy-start = (bf16[128,4096]{1,0:T(8,128)(2,1)}, bf16[128,4096]{1,0:T(8,128)(2,1)S(1)}, u32[]{:S(2)}) copy-start(bf16[128,4096]{1,0:T(8,128)(2,1)S(1)} %maximum_convert_fusion) | copy-start | bytes 3145732
Sparse Core Ops, SparseCore 0:
  17.5 83.4 all-gather.2
  114.1 20.5 reduce-scatter.5
  156.5 52.2 all-reduce.3
  219.3 21.4 reduce-scatter.7
  262.6 52.1 all-reduce.5
  326.9 21.4 reduce-scatter.9
  380.0 22.4 reduce-scatter.11
  424.3 52.1 all-reduce.7
  489.6 21.4 reduce-scatter.13
